TPU v7x, 256 devices: a whole 4x4x8 slice. The times are simulated.
256 devices in a mesh: dp: 32 (over z, y_hi, core), ctx: 8 (over x, y_lo).
Axes of the slice: x: 4, y: 4 (y_hi: 2, y_lo: 2; y = y_hi * 2 + y_lo), z: 8, core: 2. Of those that a mesh axis runs over, the one named last changes fastest.
Arguments:
- q_heads: bfloat16 [32, 1536, 2048], P('dp', 'ctx'), may hold values from -8 to 8
- keys: bfloat16 [32, 1536, 128], P('dp', 'ctx'), may hold values from -8 to 8
- values: bfloat16 [32, 1536, 128], P('dp', 'ctx'), may hold values from -6 to 6
- out_grad: bfloat16 [32, 1536, 2048], P('dp', 'ctx'), may hold values from -0.29882812 to 0.29882812
- hidden_in: bfloat16 [32, 1536, 16384], P('dp', 'ctx'), may hold values from -6 to 6
- doc_lengths: int32 [32, 8], P('dp'), may hold values from 1 to 576, 1536 in all within a row
- span_order: int32 [16], replicated, may hold values from 0 to 15, each once
- m_codes: int32 [16384, 256], P('dp'), may hold values from -127 to 127
- m_scales: float32 [2048], P('dp'), may hold values from 0.05 to 0.5
- v_codes: int32 [16384, 256], P('dp'), may hold values from 1 to 255
- v_scales: float32 [2048], P('dp'), may hold values from 0.05 to 1
Outputs:
- dq: bfloat16 [32, 1536, 2048], P('dp', 'ctx')
- update: float32 [16384, 256], P('dp')
- m_norm: float32 [16384, 256], P('dp')
- m_absmax: float32 [2048], P('dp')
- v_norm: float32 [16384, 256], P('dp')
- v_absmax: float32 [2048], P('dp')
Inputs may be any that keep to these rules, and one draw needn't show every extreme that they name: `doc_lengths`: each sequence's 8 lengths sum to 1536. `span_order`: each stored block names a different position block.
All inputs are finite; a program needn't handle non-finite values. Where the computation divides by a largest or mean magnitude, that divisor is 1e-20 or more.
Results may differ from a plain program's by a relative error of at most 0.0078.
Values may be sent and summed in bfloat16 or wider, within the bound.
A program may use at most 128 MiB of HBM per device.

v0:
```python
import math
import jax
import jax.numpy as jnp
from jax import lax
from jax.sharding import PartitionSpec as P

BLOCK = 2048
STEP = 10


def positions(order, span, total):
    rows = jnp.arange(total, dtype=jnp.int32)
    slot = rows // span
    match = slot[:, None] == jnp.arange(order.shape[0], dtype=jnp.int32)[None, :]
    first = jnp.sum(jnp.where(match, order[None, :], 0), axis=1)
    return first * span + rows % span


def documents(pos, lengths):
    ends = jnp.cumsum(lengths)
    return jnp.sum((pos[:, None] >= ends[None, :]).astype(jnp.int32), axis=1)


def adam_blocks(grad, m_codes, m_scales, v_codes, v_scales):
    shape = grad.shape
    g_blocks = grad.reshape(-1, BLOCK)
    m_old = m_codes.reshape(-1, BLOCK).astype(jnp.float32) / 127.0 * m_scales[:, None]
    v_old = v_codes.reshape(-1, BLOCK).astype(jnp.float32) / 255.0 * v_scales[:, None]
    moment = 0.9 * m_old + 0.1 * g_blocks
    second = 0.95 * v_old + 0.05 * g_blocks * g_blocks
    update = moment / (1.0 - 0.9**STEP) / (jnp.sqrt(second / (1.0 - 0.95**STEP)) + 1e-08)
    m_absmax = jnp.max(jnp.abs(moment), axis=1)
    v_absmax = jnp.max(second, axis=1)
    m_norm = moment / (m_absmax[:, None] + 1e-06)
    v_norm = second / (v_absmax[:, None] + 1e-06)
    return (update.reshape(shape), m_norm.reshape(shape), m_absmax, v_norm.reshape(shape), v_absmax)


def contract_rows(left, right):
    return lax.dot_general(
        left, right, (((0,), (0,)), ((), ())), preferred_element_type=jnp.float32
    )


def contract_cols(left, right):
    return lax.dot_general(
        left, right, (((1,), (1,)), ((), ())), preferred_element_type=jnp.float32
    )


def shards(
    q_heads,
    keys,
    values,
    out_grad,
    hidden_in,
    doc_lengths,
    span_order,
    m_codes,
    m_scales,
    v_codes,
    v_scales,
):
    rows = q_heads.shape[1]
    head_dim = keys.shape[2]
    heads_width = q_heads.shape[2]
    nheads = heads_width // head_dim
    scale = 1.0 / math.sqrt(head_dim)
    total = rows * lax.axis_size("ctx")
    key_all, value_all = (
        lax.all_gather(keys[0], "ctx", axis=0, tiled=True),
        lax.all_gather(values[0], "ctx", axis=0, tiled=True),
    )
    pos = positions(span_order, rows // 2, total)
    doc = documents(pos, doc_lengths[0])
    first_row = lax.axis_index("ctx") * rows
    query_pos = lax.dynamic_slice_in_dim(pos, first_row, rows)
    query_doc = lax.dynamic_slice_in_dim(doc, first_row, rows)
    queries = q_heads[0].reshape(rows * nheads, head_dim)
    grads_out = out_grad[0].reshape(rows * nheads, head_dim)
    width = min(512, total)
    nblocks = total // width
    blocks = (
        key_all.reshape(nblocks, width, head_dim),
        value_all.reshape(nblocks, width, head_dim),
        pos.reshape(nblocks, width),
        doc.reshape(nblocks, width),
    )

    def block_masks(key_pos, key_doc):
        small = (key_pos[None, :] <= query_pos[:, None]) & (key_doc[None, :] == query_doc[:, None])
        wide = jnp.broadcast_to(small[:, None, :], (rows, nheads, width)).reshape(
            rows * nheads, width
        )
        return (small, wide)

    def forward_terms(carry, block):
        key_block, value_block, key_pos, key_doc = block
        small, wide = block_masks(key_pos, key_doc)
        top, denom, weighted = carry
        scores = contract_cols(queries, key_block) * scale
        dprob = contract_cols(grads_out, value_block)
        new_top = jnp.maximum(top, jnp.max(jnp.where(wide, scores, -1e30), axis=1, keepdims=True))
        expo = jnp.where(wide, jnp.exp(scores - new_top), 0.0)
        factor = jnp.exp(top - new_top)
        result = (
            new_top,
            denom * factor + jnp.sum(expo, axis=1, keepdims=True),
            weighted * factor + jnp.sum(expo * dprob, axis=1, keepdims=True),
        )
        return (result, None)

    column = jnp.zeros((rows * nheads, 1), jnp.float32)
    start_state = (column - 1e30, column, column)
    (top, denom, weighted), unused = lax.scan(forward_terms, start_state, blocks)
    delta = weighted / denom

    def backward_terms(accum, block):
        key_block, value_block, key_pos, key_doc = block
        small, wide = block_masks(key_pos, key_doc)
        acc = accum
        scores = contract_cols(queries, key_block) * scale
        dprob = contract_cols(grads_out, value_block)
        prob = jnp.where(wide, jnp.exp(scores - top), 0.0) / denom
        prob_low = prob.astype(jnp.bfloat16)
        dscore = (prob * (dprob - delta)).astype(jnp.bfloat16)
        acc = acc + jnp.dot(dscore, key_block, preferred_element_type=jnp.float32)
        dkey = contract_rows(dscore, queries) * scale
        dvalue = contract_rows(prob_low, grads_out)
        return (acc, jnp.concatenate([dkey, dvalue], axis=1))

    dq_sum, pieces = lax.scan(
        backward_terms, jnp.zeros((rows * nheads, head_dim), jnp.float32), blocks
    )
    dq = (dq_sum * scale).reshape(1, rows, heads_width).astype(jnp.bfloat16)
    partial_grads = pieces.reshape(total, 2 * head_dim)
    own = lax.psum_scatter(partial_grads, "ctx", scatter_dimension=0, tiled=True)
    own_low = own.astype(jnp.bfloat16)
    layer_in = hidden_in[0]
    grad = lax.psum_scatter(contract_rows(layer_in, own_low), "dp", scatter_dimension=0, tiled=True)
    grad = lax.psum(grad, "ctx")
    update, m_norm, m_absmax, v_norm, v_absmax = adam_blocks(
        grad, m_codes, m_scales, v_codes, v_scales
    )
    return (dq, update, m_norm, m_absmax, v_norm, v_absmax)


def solution(mesh):
    in_specs = (
        P("dp", "ctx", None),
        P("dp", "ctx", None),
        P("dp", "ctx", None),
        P("dp", "ctx", None),
        P("dp", "ctx", None),
        P("dp", None),
        P(),
        P("dp", None),
        P("dp"),
        P("dp", None),
        P("dp"),
    )
    out_specs = (
        P("dp", "ctx", None),
        P("dp", None),
        P("dp", None),
        P("dp"),
        P("dp", None),
        P("dp"),
    )
    return jax.shard_map(shards, mesh=mesh, in_specs=in_specs, out_specs=out_specs, check_vma=False)
```

profile of v0, /device:TPU:32, one launch (start us, length us, event | category | flops | bytes accessed | tf_op | source)
XLA Modules:
  0.0 549.1 jit_solution(15692817767166467675)
XLA Ops:
  11.0 29.1 %all-gather = bf16[1,1536,128]{2,1,0:T(8,128)(2,1)S(1)} all-gather(bf16[1,192,128]{2,1,0:T(8,128)(2,1)} %param.16), channel_id=2, replica_groups=mesh['dp'=32,'ctx'=8] {'ctx'}, dimensions={1}, use_global_device_ids=true | all-gather | bytes 442368 | tf_op jit(solution)/shard_map/all_gather | solution.py:71
  40.1 1.4 reshape_squeeze.6
  41.5 30.8 %all-gather.1 = bf16[1,1536,128]{2,1,0:T(8,128)(2,1)} all-gather(bf16[1,192,128]{2,1,0:T(8,128)(2,1)} %param.17), channel_id=3, replica_groups=mesh['dp'=32,'ctx'=8] {'ctx'}, dimensions={1}, use_global_device_ids=true | all-gather | bytes 442368 | tf_op jit(solution)/shard_map/all_gather | solution.py:72
  72.7 46.8 %while.28 = (s32[]{:T(128)}, f32[3072,1]{0,1:T(1,128)}, f32[3072,1]{0,1:T(1,128)}, f32[3072,1]{0,1:T(1,128)}, s32[3,512]{1,0:T(4,128)}, /*index=5*/s32[192]{0:T(...) while((s32[]{:T(128)}, f32[3072,1]{0,1:T(1,128)}, ...), condition=%wide.region_7.8_spmd.clone, body=%wide.region_3.7_spmd.clone.sunk | while | flops 824497152 | bytes 55990092 | solution.py:115
  74.7 1.7 copy.45
  76.4 3.9 fusion.79
  80.3 5.2 fusion.81
  85.5 1.6 fusion.82
  89.8 1.7 copy.45
  91.5 3.9 fusion.79
  96.1 5.2 fusion.81
  101.3 1.6 fusion.82
  105.6 1.7 copy.45
  107.3 3.8 fusion.79
  111.9 5.2 fusion.81
  117.1 1.6 fusion.82
  119.5 1.3 div.70
  120.9 55.8 %while.29 = (s32[]{:T(128)}, f32[3072,128]{1,0:T(8,128)}, f32[3,512,256]{2,1,0:T(8,128)}, s32[3,512]{1,0:T(4,128)}, s32[192]{0:T(256)S(1)}, /*index=5*/s32[3,512...) while((s32[]{:T(128)}, f32[3072,128]{1,0:T(8,128)}, ...), condition=%wide.region_9.10_spmd.clone, body=%wide.region_8.9_spmd.clone.sunk | while | flops 2027126784 | bytes 108267456 | solution.py:132
  123.0 1.7 copy.46
  124.7 1.9 fusion.94
  126.7 2.9 fusion.95
  129.7 2.2 convolution_add_fusion.2
  131.9 1.1 copy-done.2
  133.0 2.3 fusion.96
  135.3 2.3 convolution_multiply_fusion.2
  139.2 0.9 constant_dynamic-slice_fusion.7
  141.3 1.7 copy.46
  143.0 1.9 fusion.94
  145.0 2.9 fusion.95
  148.0 3.8 convolution_add_fusion.2
  151.7 2.3 fusion.96
  154.1 2.3 convolution_multiply_fusion.2
  157.9 0.9 constant_dynamic-slice_fusion.7
  160.0 1.7 copy.46
  161.8 1.9 fusion.94
  163.7 2.9 fusion.95
  166.7 3.8 convolution_add_fusion.2
  170.5 2.3 fusion.96
  172.8 2.3 convolution_multiply_fusion.2
  176.7 49.4 %reduce-scatter.3.cloned.1.call-done = f32[192,256]{1,0:T(8,128)} async-done(((f32[1536,256]{1,0:T(8,128)}), f32[192,256]{1,0:T(8,128)}) %reduce-scatter.3.cloned.1.call-update) | async-done | bytes 196624 | tf_op jit(solution)/shard_map/reduce_scatter | solution.py:137
  226.2 11.0 %convolution_bitcast_fusion = f32[16384,256]{0,1:T(8,128)} fusion(bf16[1,192,16384]{2,1,0:T(8,128)(2,1)} %param.19, f32[192,256]{1,0:T(8,128)} %reduce-scatter.3.cloned.1.call-done), kind=kOutput, calls=%fused_computation.49 | convolution fusion | flops 1610661888 | bytes 23265280 | tf_op jit(solution)/shard_map/dot_general | solution.py:40
  237.3 218.4 %reduce-scatter.5.cloned.1.call-done = f32[512,256]{0,1:T(8,128)} async-done(((f32[16384,256]{0,1:T(8,128)}), f32[512,256]{0,1:T(8,128)}) %reduce-scatter.5.cloned.1.call-update) | async-done | bytes 524304 | tf_op jit(solution)/shard_map/reduce_scatter | solution.py:140
  455.9 1.2 convert_element_type.40
  457.9 79.3 %all-reduce.2.cloned.1.call-done = f32[512,256]{0,1:T(8,128)} async-done(((f32[512,256]{0,1:T(8,128)}), f32[512,256]{0,1:T(8,128)}) %all-reduce.2.cloned.1.call-update) | async-done | bytes 524304 | tf_op jit(solution)/shard_map/psum | solution.py:141
  537.2 1.3 abs_reduce_fusion
  539.6 1.0 copy.37
  540.6 1.0 copy.38
  541.6 1.0 copy.39
  (181 shorter events, 24.7 us)
Async XLA Ops:
  7.2 65.2 %copy-start.10 = (bf16[1,192,2048]{2,1,0:T(8,128)(2,1)S(1)}, bf16[1,192,2048]{2,1,0:T(8,128)(2,1)}, u32[]{:S(2)}) copy-start(bf16[1,192,2048]{2,1,0:T(8,128)(2,1)} %param.18) | copy-start | bytes 2359300
  7.2 219.0 %reduce-scatter.3.cloned.1.call-start = ((), (), s32[]{:S(2)}) async-start(), calls=%async_computation.2 | async-start | bytes 1769472 | tf_op jit(solution)/shard_map/reduce_scatter | solution.py:137
  80.3 5.2 copy-start
  85.4 1.7 copy-start.8
  85.5 1.7 copy-start.14
  85.5 1.7 copy-start.17
  96.1 5.2 copy-start
  101.3 1.7 copy-start.8
  101.3 1.7 copy-start.14
  101.3 1.7 copy-start.17
  111.9 5.2 copy-start
  117.1 1.7 copy-start.8
  117.1 1.7 copy-start.14
  117.1 1.7 copy-start.17
  120.9 5.8 %copy-start.4 = (bf16[3072,128]{1,0:T(8,128)(2,1)}, bf16[3072,128]{1,0:T(8,128)(2,1)S(1)}, u32[]{:S(2)}) copy-start(bf16[3072,128]{1,0:T(8,128)(2,1)S(1)} %get-tuple-element.577) | copy-start | bytes 2359300 | tf_op jit(solution)/shard_map/while
  120.9 5.8 %copy-start.6 = (bf16[3072,128]{1,0:T(8,128)(2,1)}, bf16[3072,128]{1,0:T(8,128)(2,1)S(1)}, u32[]{:S(2)}) copy-start(bf16[3072,128]{1,0:T(8,128)(2,1)S(1)} %get-tuple-element.581) | copy-start | bytes 2359300 | tf_op jit(solution)/shard_map/while
  120.9 3.8 copy-start.9
  120.9 3.8 copy-start.16
  124.7 2.0 copy-start.13
  126.7 3.0 copy-start.1
  129.7 3.4 copy-start.2
  137.6 1.1 copy-start.5
  137.6 1.6 copy-start.7
  139.2 5.8 %copy-start.4 = (bf16[3072,128]{1,0:T(8,128)(2,1)}, bf16[3072,128]{1,0:T(8,128)(2,1)S(1)}, u32[]{:S(2)}) copy-start(bf16[3072,128]{1,0:T(8,128)(2,1)S(1)} %get-tuple-element.577) | copy-start | bytes 2359300 | tf_op jit(solution)/shard_map/while
  139.2 5.8 %copy-start.6 = (bf16[3072,128]{1,0:T(8,128)(2,1)}, bf16[3072,128]{1,0:T(8,128)(2,1)S(1)}, u32[]{:S(2)}) copy-start(bf16[3072,128]{1,0:T(8,128)(2,1)S(1)} %get-tuple-element.581) | copy-start | bytes 2359300 | tf_op jit(solution)/shard_map/while
  139.2 3.8 copy-start.9
  139.2 3.8 copy-start.16
  143.0 2.0 copy-start.13
  145.0 3.0 copy-start.1
  148.0 3.8 copy-start.2
  156.4 1.6 copy-start.7
  157.9 5.8 %copy-start.4 = (bf16[3072,128]{1,0:T(8,128)(2,1)}, bf16[3072,128]{1,0:T(8,128)(2,1)S(1)}, u32[]{:S(2)}) copy-start(bf16[3072,128]{1,0:T(8,128)(2,1)S(1)} %get-tuple-element.577) | copy-start | bytes 2359300 | tf_op jit(solution)/shard_map/while
  157.9 5.8 %copy-start.6 = (bf16[3072,128]{1,0:T(8,128)(2,1)}, bf16[3072,128]{1,0:T(8,128)(2,1)S(1)}, u32[]{:S(2)}) copy-start(bf16[3072,128]{1,0:T(8,128)(2,1)S(1)} %get-tuple-element.581) | copy-start | bytes 2359300 | tf_op jit(solution)/shard_map/while
  157.9 3.8 copy-start.9
  157.9 3.8 copy-start.16
  161.7 2.0 copy-start.13
  163.7 3.0 copy-start.1
  166.7 3.8 copy-start.2
  175.1 1.6 copy-start.7
  176.7 279.0 %reduce-scatter.5.cloned.1.call-start = ((), (), s32[]{:S(2)}) async-start(), calls=%async_computation.3 | async-start | bytes 17301504 | tf_op jit(solution)/shard_map/reduce_scatter | solution.py:140
  237.2 218.6 %copy-start.3 = (f32[3072,128]{1,0:T(8,128)S(1)}, f32[3072,128]{1,0:T(8,128)}, u32[]{:S(2)}) copy-start(f32[3072,128]{1,0:T(8,128)} %get-tuple-element.146) | copy-start | bytes 4718596
  237.2 219.9 %copy-start.21 = (f32[64]{0:T(128)S(1)}, f32[64]{0:T(128)}, u32[]{:S(2)}) copy-start(f32[64]{0:T(128)} %param.23) | copy-start | bytes 772
  237.2 220.1 %copy-start.11 = (s32[512,256]{1,0:T(8,128)S(1)}, s32[512,256]{1,0:T(8,128)}, u32[]{:S(2)}) copy-start(s32[512,256]{1,0:T(8,128)} %param.22) | copy-start | bytes 1572868
  237.2 220.3 %copy-start.22 = (f32[64]{0:T(128)S(1)}, f32[64]{0:T(128)}, u32[]{:S(2)}) copy-start(f32[64]{0:T(128)} %param.25) | copy-start | bytes 772
  237.2 220.4 %copy-start.12 = (s32[512,256]{1,0:T(8,128)S(1)}, s32[512,256]{1,0:T(8,128)}, u32[]{:S(2)}) copy-start(s32[512,256]{1,0:T(8,128)} %param.24) | copy-start | bytes 1572868
  237.2 300.0 %all-reduce.2.cloned.1.call-start = ((), (), s32[]{:S(2)}) async-start(), calls=%async_computation.4 | async-start | bytes 1048576 | tf_op jit(solution)/shard_map/psum | solution.py:141
  538.7 3.9 copy-start.19
  539.1 3.5 copy-start.20
  (8 other events, 6.0 us)
Sparse Core Ops, SparseCore 0:
  176.8 49.3 reduce-scatter.2
  237.3 218.3 reduce-scatter.4
  458.5 78.6 all-reduce.1
where the time goes:
time: 550 us; the launch traced here: 549 us
  waiting for transfers between devices  347 us (63%)
  matrix products  76.2 us (14%)
  blocking collectives  59.9 us (11%)
  local copies, waits for them, and re-layouts  33.6 us (6%)
  other arithmetic  17.2 us (3%)
  between operations  14 us (3%)
    reduce_scatter x1, waiting for transfers between devices, shards(): lax.psum_scatter(contract_rows(layer_in, own_low), 'dp', scatter_dimensio...  218 us
    psum x1, waiting for transfers between devices, shards(): grad = lax.psum(grad, 'ctx')  79.3 us
    reduce_scatter x1, waiting for transfers between devices, shards(): lax.psum_scatter(partial_grads, 'ctx', scatter_dimension=0, tiled=True)  49.4 us
    dot_general x12, matrix products, contract_cols(): lax.dot_general(left, right, (((1,), (1,)), ((), ())), preferred_element_...  41.6 us
    all_gather x1, blocking collectives, shards(): lax.all_gather(values[0], 'ctx', axis=0, tiled=True)  30.8 us
    all_gather x1, blocking collectives, shards(): lax.all_gather(keys[0], 'ctx', axis=0, tiled=True)  29.1 us
    dot_general x7, matrix products, contract_rows(): lax.dot_general(left, right, (((0,), (0,)), ((), ())), preferred_element_...  24.8 us
  transfers between devices with their start and end apart: 3, of which 3 were waited for; matrix products, arithmetic and copies ran while one was open for 0% of the time, Pallas kernels for 0%

commit v1 on v0

--- a/solution.py
+++ b/solution.py
@@ -138,7 +138,7 @@
     own_low = own.astype(jnp.bfloat16)
     layer_in = hidden_in[0]
     grad = lax.psum_scatter(contract_rows(layer_in, own_low), "dp", scatter_dimension=0, tiled=True)
-    grad = lax.psum(grad, "ctx")
+    grad = jnp.sum(lax.all_gather(grad, "ctx"), axis=0)
     update, m_norm, m_absmax, v_norm, v_absmax = adam_blocks(
         grad, m_codes, m_scales, v_codes, v_scales
     )

time: 550 us -> 578 us (1.051)
  waiting for transfers between devices: 347 us -> 359 us
  matrix products: 76.2 us -> 83.3 us
    all_gather x0 -> x1, waiting for transfers between devices: none -> 91.1 us  [shards(): grad = jnp.sum(lax.all_gather(grad, 'ctx'), axis=0)]
    psum x1 -> x0, waiting for transfers between devices: 79.3 us -> none  [shards(): grad = lax.psum(grad, 'ctx')]
    dot_general x12, matrix products: 41.6 us -> 48.8 us  [contract_cols(): lax.dot_general(left, right, (((1,), (1,)), ((), ())), preferred_element_...]
    unnamed x21 -> x20, local copies, waits for them, and re-layouts: 3.42 us -> 9.4 us
where the time goes in v1:
time: 578 us; the launch traced here: 574 us
  waiting for transfers between devices  359 us (62%)
  matrix products  83.3 us (14%)
  blocking collectives  59.9 us (10%)
  local copies, waits for them, and re-layouts  38.4 us (7%)
  other arithmetic  18.9 us (3%)
  between operations  14 us (2%)
    reduce_scatter x1, waiting for transfers between devices, shards(): lax.psum_scatter(contract_rows(layer_in, own_low), 'dp', scatter_dimensio...  219 us
    all_gather x1, waiting for transfers between devices, shards(): grad = jnp.sum(lax.all_gather(grad, 'ctx'), axis=0)  91.1 us
    reduce_scatter x1, waiting for transfers between devices, shards(): lax.psum_scatter(partial_grads, 'ctx', scatter_dimension=0, tiled=True)  49.2 us
    dot_general x12, matrix products, contract_cols(): lax.dot_general(left, right, (((1,), (1,)), ((), ())), preferred_element_...  48.8 us
    all_gather x1, blocking collectives, shards(): lax.all_gather(values[0], 'ctx', axis=0, tiled=True)  30.8 us
    all_gather x1, blocking collectives, shards(): lax.all_gather(keys[0], 'ctx', axis=0, tiled=True)  29.1 us
    dot_general x7, matrix products, contract_rows(): lax.dot_general(left, right, (((0,), (0,)), ((), ())), preferred_element_...  24.8 us
  transfers between devices with their start and end apart: 3, of which 3 were waited for; matrix products, arithmetic and copies ran while one was open for 0% of the time, Pallas kernels for 0%

profile of v1, /device:TPU:32, one launch (start us, length us, event | category | flops | bytes accessed | tf_op | source)
XLA Modules:
  0.0 574.3 jit_solution(10893409055551548766)
XLA Ops:
  10.9 29.1 %all-gather = bf16[1,1536,128]{2,1,0:T(8,128)(2,1)S(1)} all-gather(bf16[1,192,128]{2,1,0:T(8,128)(2,1)} %param.16), channel_id=2, replica_groups=mesh['dp'=32,'ctx'=8] {'ctx'}, dimensions={1}, use_global_device_ids=true | all-gather | bytes 442368 | tf_op jit(solution)/shard_map/all_gather | solution.py:71
  40.0 2.2 reshape_squeeze.6
  42.2 30.8 %all-gather.1 = bf16[1,1536,128]{2,1,0:T(8,128)(2,1)} all-gather(bf16[1,192,128]{2,1,0:T(8,128)(2,1)} %param.17), channel_id=3, replica_groups=mesh['dp'=32,'ctx'=8] {'ctx'}, dimensions={1}, use_global_device_ids=true | all-gather | bytes 442368 | tf_op jit(solution)/shard_map/all_gather | solution.py:72
  73.0 2.2 reshape_squeeze.7
  75.2 50.5 %while.28 = (s32[]{:T(128)}, f32[3072,1]{0,1:T(1,128)S(1)}, f32[3072,1]{0,1:T(1,128)}, f32[3072,1]{0,1:T(1,128)S(1)}, s32[3,512]{1,0:T(4,128)}, /*index=5*/s32[1...) while((s32[]{:T(128)}, f32[3072,1]{0,1:T(1,128)S(1)}, ...), condition=%wide.region_7.8_spmd.clone, body=%wide.region_3.7_spmd.clone.sunk | while | flops 824497152 | bytes 55744192 | solution.py:115
  77.2 1.7 copy.46
  78.9 5.0 fusion.79
  83.9 5.4 fusion.81
  89.3 1.6 fusion.82
  93.6 1.7 copy.46
  95.3 5.0 fusion.79
  100.3 5.3 fusion.81
  105.7 1.6 fusion.82
  107.3 1.4 fusion.83
  110.6 1.7 copy.46
  112.3 5.0 fusion.79
  117.4 5.4 fusion.81
  122.7 1.6 fusion.82
  124.4 1.4 fusion.83
  125.8 1.3 div.70
  127.1 56.8 %while.29 = (s32[]{:T(128)}, f32[3072,128]{1,0:T(8,128)}, f32[3,512,256]{2,1,0:T(8,128)}, s32[3,512]{1,0:T(4,128)}, s32[192]{0:T(256)S(1)}, /*index=5*/s32[3,512...) while((s32[]{:T(128)}, f32[3072,128]{1,0:T(8,128)}, ...), condition=%wide.region_9.10_spmd.clone, body=%wide.region_8.9_spmd.clone.sunk | while | flops 2027126784 | bytes 95536888 | solution.py:132
  129.1 1.7 copy.47
  130.8 3.1 fusion.94
  133.9 2.8 fusion.95
  136.7 2.2 convolution_add_fusion.2
  138.9 1.2 copy-done.2
  140.0 2.3 fusion.96
  142.4 2.3 convolution_multiply_fusion.2
  147.7 1.7 copy.47
  149.4 3.1 fusion.94
  152.5 2.8 fusion.95
  155.4 3.7 convolution_add_fusion.2
  159.1 2.3 fusion.96
  161.4 2.3 convolution_multiply_fusion.2
  166.8 1.7 copy.47
  168.5 3.1 fusion.94
  171.6 2.8 fusion.95
  174.5 3.7 convolution_add_fusion.2
  178.2 2.3 fusion.96
  180.5 2.3 convolution_multiply_fusion.2
  184.0 49.2 %reduce-scatter.3.cloned.1.call-done = f32[192,256]{1,0:T(8,128)} async-done(((f32[1536,256]{1,0:T(8,128)}), f32[192,256]{1,0:T(8,128)}) %reduce-scatter.3.cloned.1.call-update) | async-done | bytes 196624 | tf_op jit(solution)/shard_map/reduce_scatter | solution.py:137
  233.2 11.0 %convolution_bitcast_fusion = f32[16384,256]{0,1:T(8,128)} fusion(bf16[1,192,16384]{2,1,0:T(8,128)(2,1)} %param.19, f32[192,256]{1,0:T(8,128)} %reduce-scatter.3.cloned.1.call-done), kind=kOutput, calls=%fused_computation.49 | convolution fusion | flops 1610661888 | bytes 23265280 | tf_op jit(solution)/shard_map/dot_general | solution.py:40
  244.5 218.7 %reduce-scatter.5.cloned.1.call-done = f32[512,256]{0,1:T(8,128)} async-done(((f32[16384,256]{0,1:T(8,128)}), f32[512,256]{0,1:T(8,128)}) %reduce-scatter.5.cloned.1.call-update) | async-done | bytes 524304 | tf_op jit(solution)/shard_map/reduce_scatter | solution.py:140
  463.4 1.2 convert_element_type.40
  465.4 91.1 %all-gather.5.cloned.1.call-done = f32[4096,256]{0,1:T(8,128)} async-done(((f32[512,256]{0,1:T(8,128)}), f32[4096,256]{0,1:T(8,128)}) %all-gather.5.cloned.1.call-update) | async-done | bytes 4194320 | tf_op jit(solution)/shard_map/all_gather | solution.py:141
  556.5 6.0 %copy.42 = f32[32,8,8,512]{3,2,1,0:T(8,128)S(1)} copy(f32[32,8,8,512]{3,1,2,0:T(8,128)} %bitcast.150) | data formatting | bytes 8388608
  562.5 1.0 bitcast_reduce_fusion
  564.8 1.0 copy.36
  (109 shorter events, 23.8 us)
Async XLA Ops:
  7.2 226.0 %reduce-scatter.3.cloned.1.call-start = ((), (), s32[]{:S(2)}) async-start(), calls=%async_computation.2 | async-start | bytes 1769472 | tf_op jit(solution)/shard_map/reduce_scatter | solution.py:137
  83.9 5.4 copy-start
  100.3 5.4 copy-start
  117.4 5.4 copy-start
  133.8 2.8 copy-start.1
  136.7 3.4 copy-start.2
  152.5 2.8 copy-start.1
  155.4 3.8 copy-start.2
  171.6 2.8 copy-start.1
  174.5 3.8 copy-start.2
  183.9 279.3 %reduce-scatter.5.cloned.1.call-start = ((), (), s32[]{:S(2)}) async-start(), calls=%async_computation.3 | async-start | bytes 17301504 | tf_op jit(solution)/shard_map/reduce_scatter | solution.py:140
  244.2 219.1 %copy-start.3 = (f32[3072,128]{1,0:T(8,128)S(1)}, f32[3072,128]{1,0:T(8,128)}, u32[]{:S(2)}) copy-start(f32[3072,128]{1,0:T(8,128)} %get-tuple-element.146) | copy-start | bytes 4718596
  244.2 220.4 %copy-start.8 = (f32[64]{0:T(128)S(1)}, f32[64]{0:T(128)}, u32[]{:S(2)}) copy-start(f32[64]{0:T(128)} %param.23) | copy-start | bytes 772
  244.2 220.6 %copy-start.4 = (s32[512,256]{1,0:T(8,128)S(1)}, s32[512,256]{1,0:T(8,128)}, u32[]{:S(2)}) copy-start(s32[512,256]{1,0:T(8,128)} %param.22) | copy-start | bytes 1572868
  244.2 220.8 %copy-start.9 = (f32[64]{0:T(128)S(1)}, f32[64]{0:T(128)}, u32[]{:S(2)}) copy-start(f32[64]{0:T(128)} %param.25) | copy-start | bytes 772
  244.2 220.9 %copy-start.5 = (s32[512,256]{1,0:T(8,128)S(1)}, s32[512,256]{1,0:T(8,128)}, u32[]{:S(2)}) copy-start(s32[512,256]{1,0:T(8,128)} %param.24) | copy-start | bytes 1572868
  244.2 312.2 %all-gather.5.cloned.1.call-start = ((), (), s32[]{:S(2)}) async-start(), calls=%async_computation.4 | async-start | bytes 4718592 | tf_op jit(solution)/shard_map/all_gather | solution.py:141
  563.9 3.9 copy-start.6
  564.3 3.5 copy-start.7
Sparse Core Ops, SparseCore 0:
  184.1 49.0 reduce-scatter.2
  244.3 218.8 reduce-scatter.4
  465.1 91.2 all-gather.4
